TPU v7x, 128 devices: a whole 4x4x4 slice. The times are simulated.
128 devices in a mesh: blk: 16 (over y, z), ctr: 8 (over x, core).
Axes of the slice: x: 4, y: 4, z: 4, core: 2. Of those that a mesh axis runs over, the one named last changes fastest.
Arguments:
- three_centre: bfloat16 [8, 128, 3, 1024, 128], P('ctr', None, None, 'blk'), may hold values from -6 to 6
- green_occupied: bfloat16 [8, 3, 128, 128], P('ctr'), may hold values from -0.3125 to 0.3125
- green_virtual: bfloat16 [8, 3, 128, 128], P('ctr'), may hold values from -0.3125 to 0.3125
- block_sizes: int32 [8], replicated, may hold values from 64 to 128
- screening: int32 [8, 3], replicated, may hold values 0 or 1
Outputs:
- response: float32 [1024, 1024], P(('blk', 'ctr'))
All inputs are finite; a program needn't handle non-finite values.
Results may differ from a plain program's by a relative error of at most 0.0041.
Values may be sent and summed in bfloat16 or wider, within the bound.
A program may use at most 128 MiB of HBM per device.

v0:
```python
import math

import jax
import jax.numpy as jnp
from jax import lax
from jax.sharding import PartitionSpec as P


def with_halo(value, sides, width):
    for axis, dim in sides:
        peers, length = (lax.axis_size(axis), value.shape[dim])
        up = [(i, (i + 1) % peers) for i in range(peers)]
        down = [(j, i) for i, j in up]
        last = lax.slice_in_dim(value, length - width, length, axis=dim)
        first = lax.slice_in_dim(value, 0, width, axis=dim)
        before = lax.ppermute(last, axis, up)
        after = lax.ppermute(first, axis, down)
        value = jnp.concatenate([before, value, after], axis=dim)
    return value


def per_device(three_centre, green_occupied, green_virtual, block_sizes, screening):
    atoms = three_centre.shape[0]
    width = three_centre.shape[1]
    band = three_centre.shape[2]
    share = three_centre.shape[3]
    everyone = block_sizes.shape[0]
    half = band // 2
    first_atom = lax.axis_index("ctr") * atoms
    slots = jnp.arange(width, dtype=jnp.int32)
    own_sizes = lax.dynamic_slice_in_dim(block_sizes, first_atom, atoms, 0)
    row_valid = slots[None, :] < own_sizes[:, None]
    col_sizes = jnp.stack(
        [
            lax.dynamic_slice_in_dim(jnp.roll(block_sizes, half - offset), first_atom, atoms, 0)
            for offset in range(band)
        ],
        axis=1,
    )
    col_valid = slots[None, None, :] < col_sizes[:, :, None]
    own_screen = lax.dynamic_slice_in_dim(screening, first_atom, atoms, 0)
    kept_pairs = (own_screen == 1) | (jnp.arange(band, dtype=jnp.int32) == half)[None, :]
    keep = (
        row_valid[:, :, None, None, None]
        & kept_pairs[:, None, :, None, None]
        & col_valid[:, None, :, None, :]
    )
    masked = jnp.where(keep, three_centre, jnp.zeros_like(three_centre))
    padded = with_halo(masked, (("ctr", 0),), half)
    total = jnp.zeros((atoms, width, 2 * band - 1, share, width), jnp.float32)
    for offset in range(band):
        rows = padded[offset : offset + atoms].reshape(atoms, width, band * share * width)
        term = jnp.einsum(
            "aml,alr->amr", green_occupied[:, offset], rows, preferred_element_type=jnp.float32
        )
        total = total.at[:, :, offset : offset + band].add(
            term.reshape(atoms, width, band, share, width)
        )
    half_occ = total.astype(jnp.bfloat16)
    green_cols = with_halo(green_virtual, (("ctr", 0),), half)
    pieces = []
    for column in range(band):
        columns = green_cols[column : column + atoms]
        summed = jnp.zeros((atoms, width * share, width), jnp.float32)
        for inner in range(band):
            left = half_occ[:, :, column + inner].reshape(atoms, width * share, width)
            summed = summed + jnp.einsum(
                "arl,aln->arn", left, columns[:, inner], preferred_element_type=jnp.float32
            )
        pieces.append(summed.reshape(atoms, width, share, width))
    both_half = jnp.stack(pieces, axis=2).astype(jnp.bfloat16)
    moved_tensor, moved_virtual = (
        lax.all_to_all(masked, "blk", split_axis=1, concat_axis=3, tiled=True),
        lax.all_to_all(both_half, "blk", split_axis=1, concat_axis=3, tiled=True),
    )
    partial_value = jnp.einsum(
        "amopn,amoqn->pq", moved_tensor, moved_virtual, preferred_element_type=jnp.float32
    )
    scale = -2.0 / (width * math.sqrt(everyone * band))
    summed_rows = lax.psum_scatter(partial_value, ("blk", "ctr"), scatter_dimension=0, tiled=True)
    return summed_rows * scale


def solution(mesh):
    return jax.shard_map(
        per_device,
        mesh=mesh,
        in_specs=(
            P("ctr", None, None, "blk", None),
            P("ctr", None, None, None),
            P("ctr", None, None, None),
            P(),
            P(),
        ),
        out_specs=P(("blk", "ctr"), None),
        check_vma=False,
    )
```

profile of v0, /device:TPU:1, one launch (start us, length us, event | category | flops | bytes accessed | tf_op | source)
XLA Modules:
  0.0 938.6 jit_solution(6857475714648614320)
XLA Ops:
  11.1 1.9 add_bitcast_fusion
  14.9 6.0 bitcast_select_fusion
  21.0 2.6 collective-permute-start
  23.6 1.7 collective-permute-start.2
  25.3 7.9 all-to-all-start
  33.2 10.7 %copy.43 = bf16[16,8,192,128]{3,1,2,0:T(8,128)(2,1)} copy(bf16[16,8,192,128]{3,2,1,0:T(8,128)(2,1)} %bitcast.78) | data formatting | bytes 12582912
  44.0 8.6 copy.24
  52.6 39.2 %collective-permute-done = bf16[1,128,3,64,128]{4,3,2,0,1:T(8,128)(2,1)} collective-permute-done((bf16[1,128,3,64,128]{4,3,2,0,1:T(8,128)(2,1)}, bf16[1,128,3,64,128]{4,3,2,0,1:T(8,128)(2,1)}, u32[]{:S(2)}, u32[]{:S(2)}) %collective-permute-start) | collective-permute-done | bytes 6291488 | tf_op jit(solution)/shard_map/ppermute | solution.py:16
  91.8 9.0 copy.39
  100.8 4.7 fusion.11
  105.6 7.5 scatter-add.10
  113.1 11.0 %fusion.1 = f32[1,128,5,64,128]{4,1,3,2,0:T(8,128)} fusion(f32[1,128,5,64,128]{4,1,3,2,0:T(8,128)} %scatter-add.10, bf16[3,64,128,128]{3,2,1,0:T(8,128)(2,1)S(1)} %bitcast.146, bf16[1,3,128,128]{3,2,1,0:T(8,128)(2,1)S(1)} %copy-done.1), kind=kOutput, calls=%fused_computation.3 | convolution fusion | flops 808452096 | bytes 31490048 | tf_op jit(solution)/shard_map/aml,alr->amr/dot_general | solution.py:53
  124.1 9.1 copy.40
  133.2 12.7 %fusion = f32[1,128,5,64,128]{4,1,3,2,0:T(8,128)} fusion(f32[1,128,5,64,128]{4,1,3,2,0:T(8,128)} %fusion.1, bf16[1,128,3,64,128]{1,4,3,2,0:T(8,128)(2,1)} %copy.40, bf16[1,3,128,128]{3,2,1,0:T(8,128)(2,1)S(1)} %copy-done.1), kind=kOutput, calls=%fused_computation.1 | convolution fusion | flops 808452096 | bytes 31490048 | tf_op jit(solution)/shard_map/aml,alr->amr/dot_general | solution.py:53
  145.9 8.2 convert_element_type.12
  154.0 2.2 fusion.35
  169.6 3.2 pad_maximum_fusion
  172.8 7.8 all-to-all-start.1
  180.6 7.6 copy.22
  188.2 71.0 %all-to-all-done.1 = bf16[1,128,3,64,128]{4,3,2,0,1:T(8,128)(2,1)} async-done(((bf16[1,128,3,64,128]{4,3,2,0,1:T(8,128)(2,1)}), bf16[1,128,3,64,128]{4,3,2,0,1:T(8,128)(2,1)}, u32[]{:S(2)}, u32[]{:S(2)}) %all-to-all-start.1) | async-done | bytes 6291488 | tf_op jit(solution)/shard_map/all_to_all | solution.py:74
  259.2 4.5 copy.34
  263.8 8.2 convolution_bitcast_fusion
  272.1 658.3 %reduce-scatter.2.cloned.1.call-done = f32[8,1024]{1,0:T(8,128)} async-done(((f32[1024,1024]{1,0:T(8,128)}), f32[8,1024]{1,0:T(8,128)}) %reduce-scatter.2.cloned.1.call-update) | async-done | bytes 32784 | tf_op jit(solution)/shard_map/reduce_scatter | solution.py:80
  930.4 1.4 broadcast_multiply_fusion
  (43 shorter events, 19.9 us)
Async XLA Ops:
  14.9 8.7 copy-start.2
  21.0 70.8 %collective-permute-start = (bf16[1,128,3,64,128]{4,3,2,0,1:T(8,128)(2,1)}, bf16[1,128,3,64,128]{4,3,2,0,1:T(8,128)(2,1)}, u32[]{:S(2)}, u32[]{:S(2)}) collective-permute-start(bf16[1,128,3,64,128]{4,3,2,0,1:T(8,128)(2,1)} %bitcast_select_fusion), channel_id=1, source_target_pairs={{0,1},{1,2},{2,3},{3,4},{4,5},{5,6},{6,7},{7,0},{8,9},{9,10},{10,1... | collective-permute-start | bytes 18874376 | tf_op jit(solution)/shard_map/ppermute | solution.py:16
  23.6 100.5 %collective-permute-start.1 = (bf16[1,128,3,64,128]{4,3,2,0,1:T(8,128)(2,1)}, bf16[1,128,3,64,128]{4,3,2,0,1:T(8,128)(2,1)}, u32[]{:S(2)}, u32[]{:S(2)}) collective-permute-start(bf16[1,128,3,64,128]{4,3,2,0,1:T(8,128)(2,1)} %bitcast_select_fusion), channel_id=1, source_target_pairs={{1,0},{2,1},{3,2},{4,3},{5,4},{6,5},{7,6},{0,7},{9,8},{10,9},{11,1... | collective-permute-start | bytes 18874376 | tf_op jit(solution)/shard_map/ppermute | solution.py:17
  23.6 136.1 %collective-permute-start.2 = (bf16[1,3,128,128]{3,2,1,0:T(8,128)(2,1)S(1)}, bf16[1,3,128,128]{3,2,1,0:T(8,128)(2,1)S(1)}, u32[]{:S(2)}, u32[]{:S(2)}) collective-permute-start(bf16[1,3,128,128]{3,2,1,0:T(8,128)(2,1)S(1)} %copy-done.2), channel_id=1, source_target_pairs={{0,1},{1,2},{2,3},{3,4},{4,5},{5,6},{6,7},{7,0},{8,9},{9,10},{10,1... | collective-permute-start | bytes 294920 | tf_op jit(solution)/shard_map/ppermute | solution.py:16
  25.3 139.8 %collective-permute-start.3 = (bf16[1,3,128,128]{3,2,1,0:T(8,128)(2,1)S(1)}, bf16[1,3,128,128]{3,2,1,0:T(8,128)(2,1)S(1)}, u32[]{:S(2)}, u32[]{:S(2)}) collective-permute-start(bf16[1,3,128,128]{3,2,1,0:T(8,128)(2,1)S(1)} %copy-done.2), channel_id=1, source_target_pairs={{1,0},{2,1},{3,2},{4,3},{5,4},{6,5},{7,6},{0,7},{9,8},{10,9},{11,1... | collective-permute-start | bytes 294920 | tf_op jit(solution)/shard_map/ppermute | solution.py:17
  25.3 147.4 %all-to-all-start = ((bf16[1,128,3,64,128]{4,3,2,0,1:T(8,128)(2,1)}), bf16[1,128,3,64,128]{4,3,2,0,1:T(8,128)(2,1)}, u32[]{:S(2)}, u32[]{:S(2)}) async-start(bf16[1,128,3,64,128]{4,3,2,0,1:T(8,128)(2,1)} %bitcast_select_fusion), calls=%async_computation | async-start | bytes 12582912 | tf_op jit(solution)/shard_map/all_to_all | solution.py:73
  52.6 48.2 %copy-start.1 = (bf16[1,3,128,128]{3,2,1,0:T(8,128)(2,1)S(1)}, bf16[1,3,128,128]{3,2,1,0:T(8,128)(2,1)}, u32[]{:S(2)}) copy-start(bf16[1,3,128,128]{3,2,1,0:T(8,128)(2,1)} %param.12) | copy-start | bytes 294916
  100.8 12.2 %slice-start = ((s8[6291456]{0:T(1024)(128)(4,1)}), s8[4194304]{0:T(1024)(128)(4,1)S(1)}, s32[]{:S(2)}) async-start(s8[6291456]{0:T(1024)(128)(4,1)} %bitcast.144), calls=%async_computation.4 | async-start | bytes 8388608
  105.6 7.5 slice-start.1
  172.8 86.5 %all-to-all-start.1 = ((bf16[1,128,3,64,128]{4,3,2,0,1:T(8,128)(2,1)}), bf16[1,128,3,64,128]{4,3,2,0,1:T(8,128)(2,1)}, u32[]{:S(2)}, u32[]{:S(2)}) async-start(bf16[1,128,3,64,128]{4,3,2,0,1:T(8,128)(2,1)} %pad_maximum_fusion), calls=%async_computation.1 | async-start | bytes 12582912 | tf_op jit(solution)/shard_map/all_to_all | solution.py:74
  180.6 749.8 %reduce-scatter.2.cloned.1.call-start = ((), (), s32[]{:S(2)}) async-start(), calls=%async_computation.3 | async-start | bytes 4227072 | tf_op jit(solution)/shard_map/reduce_scatter | solution.py:80
  259.2 4.6 copy-start
Sparse Core Ops, SparseCore 0:
  272.2 658.1 reduce-scatter.1
where the time goes:
time: 946 us; the launch traced here: 939 us
  waiting for transfers between devices  769 us (81%)
  local copies, waits for them, and re-layouts  69.5 us (7%)
  matrix products  43.1 us (5%)
  other arithmetic  23.8 us (3%)
  starting transfers between devices  20.1 us (2%)
  between operations  13.6 us (1%)
    reduce_scatter x1, waiting for transfers between devices, per_device(): lax.psum_scatter(partial_value, ('blk', 'ctr'), scatter_dimension=0, tile...  658 us
    all_to_all x1, waiting for transfers between devices, per_device(): lax.all_to_all(both_half, 'blk', split_axis=1, concat_axis=3, tiled=True)  71 us
    ppermute x2, waiting for transfers between devices, with_halo(): before = lax.ppermute(last, axis, up)  39.2 us
    dot_general x3, matrix products, per_device(): jnp.einsum('aml,alr->amr', green_occupied[:, offset], rows, preferred_ele...  28.4 us
  transfers between devices with their start and end apart: 7, of which 3 were waited for; matrix products, arithmetic and copies ran while one was open for 11% of the time, Pallas kernels for 0%

commit v1 on v0

v1 whole, which is shorter than its diff:
```python
import functools
import math

import jax
import jax.numpy as jnp
from jax import lax
from jax.experimental import pallas as pl
from jax.experimental.pallas import tpu as pltpu
from jax.sharding import PartitionSpec as P

MESH = pl.DeviceIdType.MESH
SIDE = 4
ROWS = 16

PLANE = (
    (0, 1), (0, 3), (1, 0), (3, 0),
    (1, 1), (3, 3), (1, 3), (3, 1),
    (0, 2), (2, 0), (2, 2),
    (1, 2), (3, 2), (2, 1), (2, 3),
)


def mm(a, b):
    return jnp.dot(a, b, preferred_element_type=jnp.float32)


def mm_nt(a, b):
    return lax.dot_general(a, b, (((1,), (1,)), ((), ())), preferred_element_type=jnp.float32)


def kernel(
    tc, go, gv, sizes, screen, out,
    own, halo, mrecv, bsend, brecv, gvn, gmat, gomat, vs, bsc, xsend, xrecv, ysend, yrecv,
    own_sem, slot_sem, gv_sems, halo_sems, m_sems, b_send_sem, b_recv_sem, b_own_sem,
    x_send_sem, x_recv_sem, y_send_sem, y_recv_sem,
):
    width, band, share, _ = tc.shape
    parts = share // ROWS
    nblk = mrecv.shape[0]
    nctr = lax.axis_size("ctr")
    rows = width // nblk
    blk, ctr = lax.axis_index("blk"), lax.axis_index("ctr")
    y, z = blk // SIDE, lax.rem(blk, SIDE)

    def peer(dy, dz):
        return lax.rem(y + dy, SIDE) * SIDE + lax.rem(z + dz, SIDE)

    def atom(shift):
        return lax.rem(ctr + shift + nctr, nctr)

    def send(src, dst, send_sem, recv_sem, b, c):
        pltpu.make_async_remote_copy(
            src_ref=src, dst_ref=dst, send_sem=send_sem, recv_sem=recv_sem,
            device_id=(b, c), device_id_type=MESH,
        ).start()

    def wait(ref, sem):
        pltpu.make_async_copy(ref, ref, sem).wait()

    def own_copy(part):
        slot = lax.rem(part, 2)
        return pltpu.make_async_copy(
            tc.at[:, :, pl.ds(part * ROWS, ROWS), :], own.at[slot], own_sem.at[slot]
        )

    own_copy(0).start()
    slot_copy = pltpu.make_async_copy(tc.at[pl.ds(blk * rows, rows)], mrecv.at[blk], slot_sem)
    slot_copy.start()

    barrier = pltpu.get_barrier_semaphore()
    for dy, dz in PLANE:
        pl.semaphore_signal(barrier, inc=1, device_id=(peer(dy, dz), ctr), device_id_type=MESH)
    for d in range(1, nctr):
        pl.semaphore_signal(barrier, inc=1, device_id=(blk, atom(d)), device_id_type=MESH)
    pl.semaphore_wait(barrier, len(PLANE) + nctr - 1)

    for slot, shift in ((0, 1), (1, -1)):
        send(gv, gvn.at[slot], gv_sems.at[0, slot], gv_sems.at[1, slot], blk, atom(shift))

    def first_sends(part, carry):
        piece = pl.ds(part * ROWS, ROWS)
        for slot, shift in ((0, 1), (1, -1)):
            send(
                tc.at[:, :, piece, :], halo.at[slot, part],
                halo_sems.at[0, slot, part], halo_sems.at[1, slot, part], blk, atom(shift),
            )
        for dy, dz in PLANE:
            b = peer(dy, dz)
            send(
                tc.at[pl.ds(b * rows, rows), :, piece, :], mrecv.at[blk, :, :, piece, :],
                m_sems.at[0], m_sems.at[1], b, ctr,
            )
        return carry

    lax.fori_loop(0, parts, first_sends, 0)

    r = lax.broadcasted_iota(jnp.int32, (width, width), 0)
    s = lax.broadcasted_iota(jnp.int32, (width, width), 1)
    for j in range(band):
        keep = (r < sizes[atom(0)]) & (s < sizes[atom(j - 1)])
        gomat[:, j * width : (j + 1) * width] = jnp.where(keep, go[j], jnp.zeros_like(go[j]))
    for slot in range(2):
        wait(gvn.at[slot], gv_sems.at[1, slot])
    for o in range(band):
        cols = s < sizes[atom(o - 1)]
        for j in range(band):
            for k in range(band):
                inner = j + k - o
                here = (j, pl.ds(k * width, width), pl.ds(o * width, width))
                if not 0 <= inner < band:
                    gmat[here] = jnp.zeros((width, width), gmat.dtype)
                    continue
                block = gv[inner] if o == 1 else gvn[o // 2, inner]
                keep = cols & (r < sizes[atom(j + k - 2)])
                if k != 1:
                    keep = keep & (screen[atom(j - 1), k] == 1)
                if o != 1:
                    keep = keep & (screen[atom(0), o] == 1)
                gmat[here] = jnp.where(keep, block, jnp.zeros_like(block))

    def transform(part, carry):
        slot = lax.rem(part, 2)
        own_copy(part).wait()

        @pl.when(part + 1 < parts)
        def _():
            own_copy(part + 1).start()

        step = 16
        for j in (1, 0, 2):
            if j != 1:
                wait(halo.at[j // 2, part], halo_sems.at[1, j // 2, part])

            def columns(t, carry):
                at = pl.ds(t * step, step)
                x = own[slot, at] if j == 1 else halo[j // 2, part, at]
                x = jnp.concatenate(
                    [x[:, k].reshape(step * ROWS, width) for k in range(band)], axis=1
                )
                v = mm(x, gmat[j])
                for o in range(band):
                    vs[j, o, pl.ds(t * step * ROWS, step * ROWS), :] = v[:, o * width : (o + 1) * width]
                return carry

            lax.fori_loop(0, width // step, columns, 0)

        def occupied(p, carry):
            at = pl.ds(p, width, stride=ROWS)
            right = jnp.concatenate(
                [
                    jnp.concatenate(
                        [vs[j, o, at, :].astype(jnp.bfloat16) for o in range(band)], axis=1
                    )
                    for j in range(band)
                ],
                axis=0,
            )
            b = mm(gomat[...], right)
            for o in range(band):
                bsc[o, at, :] = b[:, o * width : (o + 1) * width]
            return carry

        lax.fori_loop(0, ROWS, occupied, 0)

        def rounded(i, carry):
            for o in range(band):
                b = bsc[o, pl.ds(i * rows * ROWS, rows * ROWS), :].astype(jnp.bfloat16)
                bsend[part, i, :, o] = b.reshape(rows, ROWS, width)
            return carry

        lax.fori_loop(0, nblk, rounded, 0)
        for dy, dz in PLANE:
            b = peer(dy, dz)
            send(bsend.at[part, b], brecv.at[part, blk], b_send_sem, b_recv_sem.at[part], b, ctr)
        pltpu.make_async_copy(bsend.at[part, blk], brecv.at[part, blk], b_own_sem.at[part]).start()
        return carry

    lax.fori_loop(0, parts, transform, 0)

    slot_copy.wait()
    wait(mrecv.at[pl.ds(0, nblk - 1)], m_sems.at[1])

    def product(part, carry):
        pltpu.make_async_copy(bsend.at[part, blk], brecv.at[part, blk], b_own_sem.at[part]).wait()
        wait(brecv.at[part, pl.ds(0, nblk - 1)], b_recv_sem.at[part])
        group = 4

        def tile(t, carry):
            at = pl.ds(t * group, group)
            acc = None
            for m0 in range(0, rows, 2):
                pairs = [(m, o) for m in (m0, m0 + 1) for o in range(band)]
                left = jnp.concatenate(
                    [mrecv[at, m, o].reshape(group * share, width) for m, o in pairs], axis=1
                )
                right = jnp.concatenate(
                    [brecv[part, :, m, o].reshape(nblk * ROWS, width) for m, o in pairs], axis=1
                )
                term = mm_nt(left, right)
                acc = term if acc is None else acc + term
            acc = acc.reshape(group, nctr, 8, nblk * ROWS)
            for c in range(nctr):
                xsend[part, c, pl.ds(t * group * 8, group * 8), :] = acc[:, c].reshape(
                    group * 8, nblk * ROWS
                )
            return carry

        lax.fori_loop(0, nblk // group, tile, 0)
        for d in range(1, nctr):
            c = atom(d)
            send(xsend.at[part, c], xrecv.at[part, d - 1], x_send_sem, x_recv_sem.at[part], blk, c)

        @pl.when(part > 0)
        def _():
            reduce(part - 1)

        return carry

    def reduce(part):
        wait(xrecv.at[part], x_recv_sem.at[part])
        total = xsend[part, ctr]
        for d in range(nctr - 1):
            total = total + xrecv[part, d]
        ysend[part] = total
        for n, (dy, dz) in enumerate(PLANE):
            b = peer(dy, dz)
            send(ysend.at[part, pl.ds(b * 8, 8), :], yrecv.at[part, n], y_send_sem, y_recv_sem, b, ctr)

    lax.fori_loop(0, parts, product, 0)
    reduce(parts - 1)

    scale = -2.0 / (width * math.sqrt(nctr * band))
    wait(yrecv, y_recv_sem)
    for part in range(parts):
        total = ysend[part, pl.ds(pl.multiple_of(blk * 8, 8), 8), :]
        for n in range(nblk - 1):
            total = total + yrecv[part, n]
        out[part] = total * scale

    for slot in range(2):
        wait(gvn.at[slot], gv_sems.at[0, slot])
        for part in range(parts):
            wait(halo.at[slot, part], halo_sems.at[0, slot, part])
    wait(mrecv.at[pl.ds(0, nblk - 1)], m_sems.at[0])
    wait(brecv.at[:, pl.ds(0, nblk - 1)], b_send_sem)
    wait(xrecv, x_send_sem)
    wait(yrecv, y_send_sem)


def per_device(three_centre, green_occupied, green_virtual, block_sizes, screening):
    _, width, band, share, _ = three_centre.shape
    nblk, nctr = lax.axis_size("blk"), lax.axis_size("ctr")
    parts, rows, cols = share // ROWS, width // nblk, nblk * ROWS
    bf16, f32 = jnp.bfloat16, jnp.float32
    vmem, dma = pltpu.VMEM, pltpu.SemaphoreType.DMA
    got = pl.pallas_call(
        kernel,
        out_shape=jax.ShapeDtypeStruct((parts, 8, cols), f32),
        in_specs=[
            pl.BlockSpec(memory_space=pl.ANY),
            pl.BlockSpec(memory_space=pltpu.VMEM),
            pl.BlockSpec(memory_space=pltpu.VMEM),
            pl.BlockSpec(memory_space=pltpu.SMEM),
            pl.BlockSpec(memory_space=pltpu.SMEM),
        ],
        out_specs=pl.BlockSpec(memory_space=pltpu.VMEM),
        scratch_shapes=[
            vmem((2, width, band, ROWS, width), bf16),
            vmem((2, parts, width, band, ROWS, width), bf16),
            vmem((nblk, rows, band, share, width), bf16),
            vmem((parts, nblk, rows, band, ROWS, width), bf16),
            vmem((parts, nblk, rows, band, ROWS, width), bf16),
            vmem((2, band, width, width), bf16),
            vmem((band, band * width, band * width), bf16),
            vmem((width, band * width), bf16),
            vmem((band, band, width * ROWS, width), f32),
            vmem((band, width * ROWS, width), f32),
            vmem((parts, nctr, nblk * 8, cols), f32),
            vmem((parts, nctr - 1, nblk * 8, cols), f32),
            vmem((parts, nblk * 8, cols), f32),
            vmem((parts, nblk - 1, 8, cols), f32),
            dma((2,)),
            dma,
            dma((2, 2)),
            dma((2, 2, parts)),
            dma((2,)),
            dma,
            dma((parts,)),
            dma((parts,)),
            dma,
            dma((parts,)),
            dma,
            dma,
        ],
        compiler_params=pltpu.CompilerParams(
            collective_id=0, has_side_effects=True, vmem_limit_bytes=62 << 20
        ),
        name="response",
    )(three_centre[0], green_occupied[0], green_virtual[0], block_sizes, screening)
    got = got.reshape(parts, 8, nblk, ROWS)
    return got.transpose(1, 2, 0, 3).reshape(8, nblk * share)


def solution(mesh):
    return jax.shard_map(
        per_device,
        mesh=mesh,
        in_specs=(
            P("ctr", None, None, "blk", None),
            P("ctr", None, None, None),
            P("ctr", None, None, None),
            P(),
            P(),
        ),
        out_specs=P(("blk", "ctr"), None),
        check_vma=False,
    )
```

time: 946 us -> 182 us (0.19)
  waiting for transfers between devices: 769 us -> 0 us
  Pallas kernels: 0 us -> 178 us
  local copies, waits for them, and re-layouts: 69.5 us -> 3.26 us
  matrix products: 43.1 us -> 0 us
  other arithmetic: 23.8 us -> 0 us
  starting transfers between devices: 20.1 us -> 0 us
  between operations: 13.6 us -> 0.02 us
    reduce_scatter x1 -> x0, waiting for transfers between devices: 658 us -> none  [per_device(): lax.psum_scatter(partial_value, ('blk', 'ctr'), scatter_dimension=0, tile...]
    pallas_call x0 -> x1, Pallas kernels: none -> 178 us  [per_device(): pl.pallas_call(kernel, out_shape=jax.ShapeDtypeStruct((parts, 8, cols), f...]
    all_to_all x2 -> x0, waiting for transfers between devices: 71 us -> none  [the longest x1 71 us: per_device(): lax.all_to_all(both_half, 'blk', split_axis=1, concat_axis=3, tiled=True)]
    dot_general x13 -> x0, matrix products: 43.1 us -> none  [the longest x3 28.4 us: per_device(): jnp.einsum('aml,alr->amr', green_occupied[:, offset], rows, preferred_ele...]
    ppermute x4 -> x0, waiting for transfers between devices: 39.2 us -> none  [the longest x2 39.2 us: with_halo(): before = lax.ppermute(last, axis, up)]
    another operation x2 -> x0, local copies, waits for them, and re-layouts: 18.1 us -> none
    all_to_all x2 -> x0, starting transfers between devices: 15.7 us -> none  [the longest x1 7.9 us: per_device(): lax.all_to_all(masked, 'blk', split_axis=1, concat_axis=3, tiled=True)]
    all_to_all x2 -> x0, local copies, waits for them, and re-layouts: 12.1 us -> none  [the longest x1 7.57 us: per_device(): lax.all_to_all(masked, 'blk', split_axis=1, concat_axis=3, tiled=True)]
  transfers between devices with their start and end apart: 7 -> 0, of which waited for: 3 -> 0; matrix products, arithmetic and copies ran while one was open for 11% -> 0% of each run, Pallas kernels for 0% -> 0%
where the time goes in v1:
time: 182 us; the launch traced here: 181 us
  Pallas kernels  178 us (98%)
  local copies, waits for them, and re-layouts  3.26 us (2%)
    pallas_call x1, Pallas kernels, per_device(): pl.pallas_call(kernel, out_shape=jax.ShapeDtypeStruct((parts, 8, cols), f...  178 us

profile of v1, /device:TPU:1, one launch (start us, length us, event | category | flops | bytes accessed | tf_op | source)
XLA Modules:
  0.0 181.3 jit_solution(8149713405128616989)
XLA Ops:
  0.0 1.3 copy.6.screen
  1.3 178.0 %response.1 = f32[4,8,256]{2,1,0:T(8,128)} custom-call(bf16[128,3,64,128]{3,2,1,0:T(8,128)(2,1)} %bitcast.4, bf16[3,128,128]{2,1,0:T(8,128)(2,1)} %bitcast.6, bf16[3,128,128]{2,1,0:T(8,128)(2,1)} %bitcast.7, s32[8]{0:T(128)} %sizes.1, s32[8,3]{1,0:T(8,128)} %copy.6.screen), custom_call_target="tpu_custom_call" | custom-call | tf_op jit(solution)/shard_map/response/pallas_call | solution.py:256
  179.4 0.9 reshape.6
  180.3 0.2 copy.7
  180.5 0.9 reshape.7

commit v2 on v1

--- a/solution.py
+++ b/solution.py
@@ -11,12 +11,13 @@
 MESH = pl.DeviceIdType.MESH
 SIDE = 4
 ROWS = 16
+TILES = 4
+LANES = 128
 
 PLANE = (
+    (2, 2), (1, 2), (3, 2), (2, 1), (2, 3),
+    (0, 2), (2, 0), (1, 1), (3, 3), (1, 3), (3, 1),
     (0, 1), (0, 3), (1, 0), (3, 0),
-    (1, 1), (3, 3), (1, 3), (3, 1),
-    (0, 2), (2, 0), (2, 2),
-    (1, 2), (3, 2), (2, 1), (2, 3),
 )
 
 
@@ -29,10 +30,11 @@
 
 
 def kernel(
-    tc, go, gv, sizes, screen, out,
-    own, halo, mrecv, bsend, brecv, gvn, gmat, gomat, vs, bsc, xsend, xrecv, ysend, yrecv,
-    own_sem, slot_sem, gv_sems, halo_sems, m_sems, b_send_sem, b_recv_sem, b_own_sem,
-    x_send_sem, x_recv_sem, y_send_sem, y_recv_sem,
+    tc, go_hbm, gv_hbm, sizes, screen, out,
+    own, halo, mrecv, bsend, brecv, go, gvn, gmat, gomat, vs, bsc,
+    xsend, xrecv, xsend_last, xrecv_last, ysend, yrecv,
+    in_sems, own_sem, slot_sem, gv_sems, halo_sems, m_sems, b_send_sem, b_recv_sem, b_own_sem,
+    x_send_sems, x_recv_sem, y_send_sem, y_recv_sem,
 ):
     width, band, share, _ = tc.shape
     parts = share // ROWS
@@ -63,6 +65,14 @@
             tc.at[:, :, pl.ds(part * ROWS, ROWS), :], own.at[slot], own_sem.at[slot]
         )
 
+    inputs = [
+        pltpu.make_async_copy(src, dst, in_sems.at[n])
+        for n, (src, dst) in enumerate(
+            ((go_hbm, go), (gv_hbm, gvn.at[1]))
+        )
+    ]
+    for copy in inputs:
+        copy.start()
     own_copy(0).start()
     slot_copy = pltpu.make_async_copy(tc.at[pl.ds(blk * rows, rows)], mrecv.at[blk], slot_sem)
     slot_copy.start()
@@ -75,7 +85,9 @@
     pl.semaphore_wait(barrier, len(PLANE) + nctr - 1)
 
     for slot, shift in ((0, 1), (1, -1)):
-        send(gv, gvn.at[slot], gv_sems.at[0, slot], gv_sems.at[1, slot], blk, atom(shift))
+        send(
+            gv_hbm, gvn.at[2 * slot], gv_sems.at[0, slot], gv_sems.at[1, slot], blk, atom(shift)
+        )
 
     def first_sends(part, carry):
         piece = pl.ds(part * ROWS, ROWS)
@@ -84,23 +96,29 @@
                 tc.at[:, :, piece, :], halo.at[slot, part],
                 halo_sems.at[0, slot, part], halo_sems.at[1, slot, part], blk, atom(shift),
             )
-        for dy, dz in PLANE:
-            b = peer(dy, dz)
-            send(
-                tc.at[pl.ds(b * rows, rows), :, piece, :], mrecv.at[blk, :, :, piece, :],
-                m_sems.at[0], m_sems.at[1], b, ctr,
-            )
+        for cut in range(2):
+            some = rows // 2
+            for dy, dz in PLANE:
+                b = peer(dy, dz)
+                send(
+                    tc.at[pl.ds(b * rows + cut * some, some), :, piece, :],
+                    mrecv.at[blk, pl.ds(cut * some, some), :, piece, :],
+                    m_sems.at[0], m_sems.at[1], b, ctr,
+                )
         return carry
 
     lax.fori_loop(0, parts, first_sends, 0)
 
     r = lax.broadcasted_iota(jnp.int32, (width, width), 0)
     s = lax.broadcasted_iota(jnp.int32, (width, width), 1)
+    for copy in inputs:
+        copy.wait()
     for j in range(band):
         keep = (r < sizes[atom(0)]) & (s < sizes[atom(j - 1)])
         gomat[:, j * width : (j + 1) * width] = jnp.where(keep, go[j], jnp.zeros_like(go[j]))
     for slot in range(2):
-        wait(gvn.at[slot], gv_sems.at[1, slot])
+        wait(gvn.at[2 * slot], gv_sems.at[1, slot])
+
     for o in range(band):
         cols = s < sizes[atom(o - 1)]
         for j in range(band):
@@ -110,13 +128,24 @@
                 if not 0 <= inner < band:
                     gmat[here] = jnp.zeros((width, width), gmat.dtype)
                     continue
-                block = gv[inner] if o == 1 else gvn[o // 2, inner]
+                block = gvn[o, inner]
                 keep = cols & (r < sizes[atom(j + k - 2)])
                 if k != 1:
-                    keep = keep & (screen[atom(j - 1), k] == 1)
+                    keep = keep & (screen[k, atom(j - 1)] == 1)
                 if o != 1:
-                    keep = keep & (screen[atom(0), o] == 1)
+                    keep = keep & (screen[o, atom(0)] == 1)
                 gmat[here] = jnp.where(keep, block, jnp.zeros_like(block))
+
+    def second_sends(part):
+        for cut in range(2):
+            some = pl.ds(cut * (rows // 2), rows // 2)
+            for dy, dz in PLANE:
+                b = peer(dy, dz)
+                send(
+                    bsend.at[part, b, some], brecv.at[part, blk, some],
+                    b_send_sem, b_recv_sem.at[part], b, ctr,
+                )
+        pltpu.make_async_copy(bsend.at[part, blk], brecv.at[part, blk], b_own_sem.at[part]).start()
 
     def transform(part, carry):
         slot = lax.rem(part, 2)
@@ -169,10 +198,11 @@
             return carry
 
         lax.fori_loop(0, nblk, rounded, 0)
-        for dy, dz in PLANE:
-            b = peer(dy, dz)
-            send(bsend.at[part, b], brecv.at[part, blk], b_send_sem, b_recv_sem.at[part], b, ctr)
-        pltpu.make_async_copy(bsend.at[part, blk], brecv.at[part, blk], b_own_sem.at[part]).start()
+
+        @pl.when(part > 0)
+        def _():
+            second_sends(part - 1)
+
         return carry
 
     lax.fori_loop(0, parts, transform, 0)
@@ -180,13 +210,20 @@
     slot_copy.wait()
     wait(mrecv.at[pl.ds(0, nblk - 1)], m_sems.at[1])
 
-    def product(part, carry):
+    group = nblk // TILES
+    cols = nblk * ROWS
+    last = parts - 1
+
+    def first(t):
+        return lax.rem(y + t, TILES) * group
+
+    def product(part, sent, got, send_sem):
         pltpu.make_async_copy(bsend.at[part, blk], brecv.at[part, blk], b_own_sem.at[part]).wait()
         wait(brecv.at[part, pl.ds(0, nblk - 1)], b_recv_sem.at[part])
-        group = 4
 
         def tile(t, carry):
-            at = pl.ds(t * group, group)
+            at = pl.ds(first(t), group)
+            here = pl.ds(pl.multiple_of(t * group * 8, group * 8), group * 8)
             acc = None
             for m0 in range(0, rows, 2):
                 pairs = [(m, o) for m in (m0, m0 + 1) for o in range(band)]
@@ -194,57 +231,94 @@
                     [mrecv[at, m, o].reshape(group * share, width) for m, o in pairs], axis=1
                 )
                 right = jnp.concatenate(
-                    [brecv[part, :, m, o].reshape(nblk * ROWS, width) for m, o in pairs], axis=1
+                    [brecv[part, :, m, o].reshape(cols, width) for m, o in pairs], axis=1
                 )
                 term = mm_nt(left, right)
                 acc = term if acc is None else acc + term
-            acc = acc.reshape(group, nctr, 8, nblk * ROWS)
+            acc = acc.reshape(group, nctr, 8, cols)
             for c in range(nctr):
-                xsend[part, c, pl.ds(t * group * 8, group * 8), :] = acc[:, c].reshape(
-                    group * 8, nblk * ROWS
+                sent[c, here, :] = acc[:, c].reshape(group * 8, cols).astype(sent.dtype)
+            for d in range(1, nctr):
+                c = atom(d)
+                send(
+                    sent.at[c, here, :], got.at[d - 1, here, :],
+                    send_sem, x_recv_sem.at[part, t], blk, c,
                 )
             return carry
 
-        lax.fori_loop(0, nblk // group, tile, 0)
-        for d in range(1, nctr):
-            c = atom(d)
-            send(xsend.at[part, c], xrecv.at[part, d - 1], x_send_sem, x_recv_sem.at[part], blk, c)
+        lax.fori_loop(0, TILES, tile, 0)
+
+    def reduce(part, sent, got):
+        def tile(t, carry):
+            here = pl.ds(pl.multiple_of(t * group * 8, group * 8), group * 8)
+            wait(got.at[:, here, :], x_recv_sem.at[part, t])
+            total = sent[ctr, here, :].astype(jnp.float32)
+            for d in range(nctr - 1):
+                total = total + got[d, here, :].astype(jnp.float32)
+            ysend[part, here, :] = total
+            for i in range(group):
+                b = first(t) + i
+                row = pl.ds(pl.multiple_of((t * group + i) * 8, 8), 8)
+
+                @pl.when(b == blk)
+                def _():
+                    yrecv[part, blk] = ysend[part, row, :]
+
+                @pl.when(b != blk)
+                def _():
+                    send(ysend.at[part, row, :], yrecv.at[part, blk], y_send_sem, y_recv_sem, b, ctr)
+
+            return carry
+
+        lax.fori_loop(0, TILES, tile, 0)
+
+    def middle(part, carry):
+        product(part, xsend.at[part], xrecv.at[part], x_send_sems.at[0])
+
+        @pl.when(part == 1)
+        def _():
+            second_sends(last)
 
         @pl.when(part > 0)
         def _():
-            reduce(part - 1)
+            reduce(part - 1, xsend.at[part - 1], xrecv.at[part - 1])
 
         return carry
 
-    def reduce(part):
-        wait(xrecv.at[part], x_recv_sem.at[part])
-        total = xsend[part, ctr]
-        for d in range(nctr - 1):
-            total = total + xrecv[part, d]
-        ysend[part] = total
-        for n, (dy, dz) in enumerate(PLANE):
-            b = peer(dy, dz)
-            send(ysend.at[part, pl.ds(b * 8, 8), :], yrecv.at[part, n], y_send_sem, y_recv_sem, b, ctr)
-
-    lax.fori_loop(0, parts, product, 0)
-    reduce(parts - 1)
+    lax.fori_loop(0, last, middle, 0)
+    product(last, xsend_last, xrecv_last, x_send_sems.at[1])
+    reduce(last - 1, xsend.at[last - 1], xrecv.at[last - 1])
+    reduce(last, xsend_last, xrecv_last)
 
     scale = -2.0 / (width * math.sqrt(nctr * band))
-    wait(yrecv, y_recv_sem)
+    wait(yrecv.at[:, pl.ds(0, nblk - 1)], y_recv_sem)
+    lane = lax.broadcasted_iota(jnp.int32, (8, LANES), 1)
+    held = [jnp.zeros((8, LANES), jnp.float32) for _ in range(nblk * share // LANES)]
     for part in range(parts):
-        total = ysend[part, pl.ds(pl.multiple_of(blk * 8, 8), 8), :]
-        for n in range(nblk - 1):
+        total = yrecv[part, 0]
+        for n in range(1, nblk):
             total = total + yrecv[part, n]
-        out[part] = total * scale
+        total = total * scale
+        for n in range(nblk):
+            at, to = n * ROWS, n * share + part * ROWS
+            piece = total[:, at // LANES * LANES : (at // LANES + 1) * LANES]
+            shift = (to - at) % LANES
+            if shift:
+                piece = pltpu.roll(piece, shift, 1)
+            here = (lane >= to % LANES) & (lane < to % LANES + ROWS)
+            held[to // LANES] = jnp.where(here, piece, held[to // LANES])
+    for n, piece in enumerate(held):
+        out[:, n * LANES : (n + 1) * LANES] = piece
 
     for slot in range(2):
-        wait(gvn.at[slot], gv_sems.at[0, slot])
+        wait(gvn.at[2 * slot], gv_sems.at[0, slot])
         for part in range(parts):
             wait(halo.at[slot, part], halo_sems.at[0, slot, part])
     wait(mrecv.at[pl.ds(0, nblk - 1)], m_sems.at[0])
     wait(brecv.at[:, pl.ds(0, nblk - 1)], b_send_sem)
-    wait(xrecv, x_send_sem)
-    wait(yrecv, y_send_sem)
+    wait(xrecv, x_send_sems.at[0])
+    wait(xrecv_last, x_send_sems.at[1])
+    wait(yrecv.at[:, pl.ds(0, nblk - 1)], y_send_sem)
 
 
 def per_device(three_centre, green_occupied, green_virtual, block_sizes, screening):
@@ -253,13 +327,13 @@
     parts, rows, cols = share // ROWS, width // nblk, nblk * ROWS
     bf16, f32 = jnp.bfloat16, jnp.float32
     vmem, dma = pltpu.VMEM, pltpu.SemaphoreType.DMA
-    got = pl.pallas_call(
+    return pl.pallas_call(
         kernel,
-        out_shape=jax.ShapeDtypeStruct((parts, 8, cols), f32),
+        out_shape=jax.ShapeDtypeStruct((8, nblk * share), f32),
         in_specs=[
             pl.BlockSpec(memory_space=pl.ANY),
-            pl.BlockSpec(memory_space=pltpu.VMEM),
-            pl.BlockSpec(memory_space=pltpu.VMEM),
+            pl.BlockSpec(memory_space=pl.ANY),
+            pl.BlockSpec(memory_space=pl.ANY),
             pl.BlockSpec(memory_space=pltpu.SMEM),
             pl.BlockSpec(memory_space=pltpu.SMEM),
         ],
@@ -270,15 +344,19 @@
             vmem((nblk, rows, band, share, width), bf16),
             vmem((parts, nblk, rows, band, ROWS, width), bf16),
             vmem((parts, nblk, rows, band, ROWS, width), bf16),
-            vmem((2, band, width, width), bf16),
+            vmem((band, width, width), bf16),
+            vmem((3, band, width, width), bf16),
             vmem((band, band * width, band * width), bf16),
             vmem((width, band * width), bf16),
             vmem((band, band, width * ROWS, width), f32),
             vmem((band, width * ROWS, width), f32),
-            vmem((parts, nctr, nblk * 8, cols), f32),
-            vmem((parts, nctr - 1, nblk * 8, cols), f32),
+            vmem((parts - 1, nctr, nblk * 8, cols), f32),
+            vmem((parts - 1, nctr - 1, nblk * 8, cols), f32),
+            vmem((nctr, nblk * 8, cols), bf16),
+            vmem((nctr - 1, nblk * 8, cols), bf16),
             vmem((parts, nblk * 8, cols), f32),
-            vmem((parts, nblk - 1, 8, cols), f32),
+            vmem((parts, nblk, 8, cols), f32),
+            dma((2,)),
             dma((2,)),
             dma,
             dma((2, 2)),
@@ -287,8 +365,8 @@
             dma,
             dma((parts,)),
             dma((parts,)),
-            dma,
-            dma((parts,)),
+            dma((2,)),
+            dma((parts, TILES)),
             dma,
             dma,
         ],
@@ -296,9 +374,7 @@
             collective_id=0, has_side_effects=True, vmem_limit_bytes=62 << 20
         ),
         name="response",
-    )(three_centre[0], green_occupied[0], green_virtual[0], block_sizes, screening)
-    got = got.reshape(parts, 8, nblk, ROWS)
-    return got.transpose(1, 2, 0, 3).reshape(8, nblk * share)
+    )(three_centre[0], green_occupied[0], green_virtual[0], block_sizes, screening.T)
 
 
 def solution(mesh):

time: 182 us -> 161 us (0.88)
  Pallas kernels: 178 us -> 159 us
  local copies, waits for them, and re-layouts: 3.26 us -> 1.38 us
    pallas_call x1, Pallas kernels: 178 us -> 159 us  [per_device(): pl.pallas_call(kernel, out_shape=jax.ShapeDtypeStruct((8, nblk * share),...]
where the time goes in v2:
time: 161 us
  Pallas kernels  159 us (99%)
    pallas_call x1, Pallas kernels, per_device(): pl.pallas_call(kernel, out_shape=jax.ShapeDtypeStruct((8, nblk * share),...  159 us

profile of v2, /device:TPU:1, one launch (start us, length us, event | category | flops | bytes accessed | tf_op | source)
XLA Modules:
  0.0 160.8 jit_solution(9138914383884327840)
XLA Ops:
  0.0 159.4 %response.1 = f32[8,1024]{1,0:T(8,128)} custom-call(bf16[128,3,64,128]{3,2,1,0:T(8,128)(2,1)} %bitcast.4, bf16[3,128,128]{2,1,0:T(8,128)(2,1)} %bitcast.5, bf16[3,128,128]{2,1,0:T(8,128)(2,1)} %bitcast.6, s32[8]{0:T(128)} %sizes.1, s32[3,8]{1,0:T(4,128)} %bitcast.7), custom_call_target="tpu_custom_call" | custom-call | tf_op jit(solution)/shard_map/response/pallas_call | solution.py:330
  159.4 1.4 copy.7

commit v3 on v2

--- a/solution.py
+++ b/solution.py
@@ -13,6 +13,7 @@
 ROWS = 16
 TILES = 4
 LANES = 128
+AT_ONCE = 4
 
 PLANE = (
     (2, 2), (1, 2), (3, 2), (2, 1), (2, 3),
@@ -31,7 +32,7 @@
 
 def kernel(
     tc, go_hbm, gv_hbm, sizes, screen, out,
-    own, halo, mrecv, bsend, brecv, go, gvn, gmat, gomat, vs, bsc,
+    own, halo, mrecv, bsend, brecv, go, gvn, gmat, gomat, ms, bsc,
     xsend, xrecv, xsend_last, xrecv_last, ysend, yrecv,
     in_sems, own_sem, slot_sem, gv_sems, halo_sems, m_sems, b_send_sem, b_recv_sem, b_own_sem,
     x_send_sems, x_recv_sem, y_send_sem, y_recv_sem,
@@ -109,32 +110,31 @@
 
     lax.fori_loop(0, parts, first_sends, 0)
 
+    wide = 2 * band - 1
+    terms = [(e, j) for e in range(wide) for j in range(band) if 0 <= e - j < band]
     r = lax.broadcasted_iota(jnp.int32, (width, width), 0)
     s = lax.broadcasted_iota(jnp.int32, (width, width), 1)
     for copy in inputs:
         copy.wait()
-    for j in range(band):
+    for n, (e, j) in enumerate(terms):
+        k = e - j
         keep = (r < sizes[atom(0)]) & (s < sizes[atom(j - 1)])
-        gomat[:, j * width : (j + 1) * width] = jnp.where(keep, go[j], jnp.zeros_like(go[j]))
+        if k != 1:
+            keep = keep & (screen[k, atom(j - 1)] == 1)
+        gomat[:, n * width : (n + 1) * width] = jnp.where(keep, go[j], jnp.zeros_like(go[j]))
     for slot in range(2):
         wait(gvn.at[2 * slot], gv_sems.at[1, slot])
 
-    for o in range(band):
-        cols = s < sizes[atom(o - 1)]
-        for j in range(band):
-            for k in range(band):
-                inner = j + k - o
-                here = (j, pl.ds(k * width, width), pl.ds(o * width, width))
-                if not 0 <= inner < band:
-                    gmat[here] = jnp.zeros((width, width), gmat.dtype)
-                    continue
-                block = gvn[o, inner]
-                keep = cols & (r < sizes[atom(j + k - 2)])
-                if k != 1:
-                    keep = keep & (screen[k, atom(j - 1)] == 1)
-                if o != 1:
-                    keep = keep & (screen[o, atom(0)] == 1)
-                gmat[here] = jnp.where(keep, block, jnp.zeros_like(block))
+    for e in range(wide):
+        for o in range(band):
+            here = (pl.ds(e * width, width), pl.ds(o * width, width))
+            if not 0 <= e - o < band:
+                gmat[here] = jnp.zeros((width, width), gmat.dtype)
+                continue
+            keep = (r < sizes[atom(e - 2)]) & (s < sizes[atom(o - 1)])
+            if o != 1:
+                keep = keep & (screen[o, atom(0)] == 1)
+            gmat[here] = jnp.where(keep, gvn[o, e - o], jnp.zeros((width, width), gmat.dtype))
 
     def second_sends(part):
         for cut in range(2):
@@ -163,33 +163,47 @@
             def columns(t, carry):
                 at = pl.ds(t * step, step)
                 x = own[slot, at] if j == 1 else halo[j // 2, part, at]
-                x = jnp.concatenate(
-                    [x[:, k].reshape(step * ROWS, width) for k in range(band)], axis=1
-                )
-                v = mm(x, gmat[j])
-                for o in range(band):
-                    vs[j, o, pl.ds(t * step * ROWS, step * ROWS), :] = v[:, o * width : (o + 1) * width]
+                for k in range(band):
+                    y = x[:, k].reshape(step * ROWS, width).astype(jnp.float32)
+                    ms[j, k, pl.ds(t * step * ROWS, step * ROWS), :] = y
                 return carry
 
             lax.fori_loop(0, width // step, columns, 0)
 
-        def occupied(p, carry):
-            at = pl.ds(p, width, stride=ROWS)
-            right = jnp.concatenate(
+        def green(g, carry):
+            places = [pl.ds(g * AT_ONCE + p, width, stride=ROWS) for p in range(AT_ONCE)]
+            half = []
+            for e in range(wide):
+                js = [n for n, (of, _) in enumerate(terms) if of == e]
+                right = jnp.concatenate(
+                    [
+                        jnp.concatenate(
+                            [
+                                ms[terms[n][1], e - terms[n][1], at, :].astype(jnp.bfloat16)
+                                for at in places
+                            ],
+                            axis=1,
+                        )
+                        for n in js
+                    ],
+                    axis=0,
+                )
+                left = gomat[:, js[0] * width : (js[-1] + 1) * width]
+                half.append(mm(left, right).astype(jnp.bfloat16))
+            left = jnp.concatenate(
                 [
-                    jnp.concatenate(
-                        [vs[j, o, at, :].astype(jnp.bfloat16) for o in range(band)], axis=1
-                    )
-                    for j in range(band)
+                    jnp.concatenate([h[:, p * width : (p + 1) * width] for h in half], axis=1)
+                    for p in range(AT_ONCE)
                 ],
                 axis=0,
             )
-            b = mm(gomat[...], right)
-            for o in range(band):
-                bsc[o, at, :] = b[:, o * width : (o + 1) * width]
+            b = mm(left, gmat[...])
+            for p, at in enumerate(places):
+                for o in range(band):
+                    bsc[o, at, :] = b[p * width : (p + 1) * width, o * width : (o + 1) * width]
             return carry
 
-        lax.fori_loop(0, ROWS, occupied, 0)
+        lax.fori_loop(0, ROWS // AT_ONCE, green, 0)
 
         def rounded(i, carry):
             for o in range(band):
@@ -346,8 +360,8 @@
             vmem((parts, nblk, rows, band, ROWS, width), bf16),
             vmem((band, width, width), bf16),
             vmem((3, band, width, width), bf16),
-            vmem((band, band * width, band * width), bf16),
-            vmem((width, band * width), bf16),
+            vmem(((2 * band - 1) * width, band * width), bf16),
+            vmem((width, band * band * width), bf16),
             vmem((band, band, width * ROWS, width), f32),
             vmem((band, width * ROWS, width), f32),
             vmem((parts - 1, nctr, nblk * 8, cols), f32),

time: 161 us -> 161 us (level)
  no operation moved by 1% of the time
where the time goes in v3:
time: 161 us
  Pallas kernels  159 us (99%)
    pallas_call x1, Pallas kernels, per_device(): pl.pallas_call(kernel, out_shape=jax.ShapeDtypeStruct((8, nblk * share),...  159 us

profile of v3, /device:TPU:1, one launch (start us, length us, event | category | flops | bytes accessed | tf_op | source)
XLA Modules:
  0.0 160.8 jit_solution(8640223999417910589)
XLA Ops:
  0.0 159.4 %response.1 = f32[8,1024]{1,0:T(8,128)} custom-call(bf16[128,3,64,128]{3,2,1,0:T(8,128)(2,1)} %bitcast.4, bf16[3,128,128]{2,1,0:T(8,128)(2,1)} %bitcast.5, bf16[3,128,128]{2,1,0:T(8,128)(2,1)} %bitcast.6, s32[8]{0:T(128)} %sizes.1, s32[3,8]{1,0:T(4,128)} %bitcast.7), custom_call_target="tpu_custom_call" | custom-call | tf_op jit(solution)/shard_map/response/pallas_call | solution.py:344
  159.4 1.4 copy.7

commit v4 on v3

--- a/solution.py
+++ b/solution.py
@@ -335,14 +335,390 @@
     wait(yrecv.at[:, pl.ds(0, nblk - 1)], y_send_sem)
 
 
-def per_device(three_centre, green_occupied, green_virtual, block_sizes, screening):
+def packed_kernel(
+    tc, go_hbm, gv_hbm, sizes, screen, out,
+    own, halo, msend, mrecv, bsend, brecv, go, gvn, gmat, gomat, sel, pgmat, ms, bsc,
+    xsend, xrecv, xsend_last, xrecv_last, ysend, yrecv,
+    in_sems, own_sem, slot_sem, gv_sems, halo_sems, m_sems, b_send_sem, b_recv_sem, b_own_sem,
+    x_send_sems, x_recv_sem, y_send_sem, y_recv_sem,
+):
+    width, band, share, _ = tc.shape
+    parts = share // ROWS
+    nblk = mrecv.shape[0]
+    nctr = lax.axis_size("ctr")
+    rows = width // nblk
+    blk, ctr = lax.axis_index("blk"), lax.axis_index("ctr")
+    y, z = blk // SIDE, lax.rem(blk, SIDE)
+
+    def peer(dy, dz):
+        return lax.rem(y + dy, SIDE) * SIDE + lax.rem(z + dz, SIDE)
+
+    def atom(shift):
+        return lax.rem(ctr + shift + nctr, nctr)
+
+    def send(src, dst, send_sem, recv_sem, b, c):
+        pltpu.make_async_remote_copy(
+            src_ref=src, dst_ref=dst, send_sem=send_sem, recv_sem=recv_sem,
+            device_id=(b, c), device_id_type=MESH,
+        ).start()
+
+    def wait(ref, sem):
+        pltpu.make_async_copy(ref, ref, sem).wait()
+
+    def own_copy(part):
+        slot = lax.rem(part, 2)
+        return pltpu.make_async_copy(
+            tc.at[:, :, pl.ds(part * ROWS, ROWS), :], own.at[slot], own_sem.at[slot]
+        )
+
+    inputs = [
+        pltpu.make_async_copy(src, dst, in_sems.at[n])
+        for n, (src, dst) in enumerate(
+            ((go_hbm, go), (gv_hbm, gvn.at[1]))
+        )
+    ]
+    for copy in inputs:
+        copy.start()
+    own_copy(0).start()
+    barrier = pltpu.get_barrier_semaphore()
+    for dy, dz in PLANE:
+        pl.semaphore_signal(barrier, inc=1, device_id=(peer(dy, dz), ctr), device_id_type=MESH)
+    for d in range(1, nctr):
+        pl.semaphore_signal(barrier, inc=1, device_id=(blk, atom(d)), device_id_type=MESH)
+
+    at = jnp.int32(0)
+    r = lax.broadcasted_iota(jnp.int32, (width, band * width), 0)
+    s = lax.broadcasted_iota(jnp.int32, (width, band * width), 1)
+    for o in range(band):
+        length = sizes[atom(o - 1)]
+        if o != 1:
+            length = jnp.where(screen[o, atom(0)] == 1, length, 0)
+        for i in range(2):
+            here = (s - r == at + i * (width // 2)) & (r < length)
+            sel[i, o * width : (o + 1) * width, :] = jnp.where(here, 1.0, 0.0).astype(sel.dtype)
+        at = at + length
+
+    def fold(even, odd):
+        cut = lambda v: [v[:, n * width : (n + 1) * width] for n in range(band)]
+        even, odd = cut(even), cut(odd)
+        return [*even[:-1], even[-1] + odd[0], *odd[1:]]
+
+    def pack(part):
+        slot = lax.rem(part, 2)
+        own_copy(part).wait()
+
+        @pl.when(part + 1 < parts)
+        def _():
+            own_copy(part + 1).start()
+
+        def some(g, carry):
+            x = own[slot, pl.ds(g * 4 * rows, 4 * rows)]
+            x = x.reshape(2 * rows, 2, band, ROWS, width)
+            even, odd = (
+                jnp.concatenate(
+                    [x[:, i, n].reshape(2 * rows * ROWS, width) for n in range(band)], axis=1
+                )
+                for i in range(2)
+            )
+            for t, v in enumerate(fold(mm(even, sel[0]), mm(odd, sel[1]))):
+                msend[part, pl.ds(g * 4, 4), :, t] = v.astype(jnp.bfloat16).reshape(
+                    4, rows // 2, ROWS, width
+                )
+            return carry
+
+        lax.fori_loop(0, nblk // 4, some, 0)
+
+    pack(jnp.int32(0))
+    pl.semaphore_wait(barrier, len(PLANE) + nctr - 1)
+
+    for slot, shift in ((0, 1), (1, -1)):
+        send(
+            gv_hbm, gvn.at[2 * slot], gv_sems.at[0, slot], gv_sems.at[1, slot], blk, atom(shift)
+        )
+
+    def first_sends(part, carry):
+        piece = pl.ds(part * ROWS, ROWS)
+        for slot, shift in ((0, 1), (1, -1)):
+            send(
+                tc.at[:, :, piece, :], halo.at[slot, part],
+                halo_sems.at[0, slot, part], halo_sems.at[1, slot, part], blk, atom(shift),
+            )
+
+        @pl.when(part > 0)
+        def _():
+            pack(part)
+
+        for cut in range(2):
+            some = pl.ds(cut * (rows // 4), rows // 4)
+            for dy, dz in PLANE:
+                b = peer(dy, dz)
+                send(
+                    msend.at[part, b, some], mrecv.at[blk, some, :, piece, :],
+                    m_sems.at[0], m_sems.at[1], b, ctr,
+                )
+        pltpu.make_async_copy(
+            msend.at[part, blk], mrecv.at[blk, :, :, piece, :], slot_sem
+        ).start()
+        return carry
+
+    lax.fori_loop(0, parts, first_sends, 0)
+    own_copy(0).start()
+
+    wide = 2 * band - 1
+    terms = [(e, j) for e in range(wide) for j in range(band) if 0 <= e - j < band]
+    r = lax.broadcasted_iota(jnp.int32, (width, width), 0)
+    s = lax.broadcasted_iota(jnp.int32, (width, width), 1)
+    for copy in inputs:
+        copy.wait()
+    half_width = width // 2
+    place = jnp.where(r < half_width, 2 * r, 2 * (r - half_width) + 1)
+    order = jnp.where(s == place, 1.0, 0.0).astype(jnp.bfloat16)
+    for n, (e, j) in enumerate(terms):
+        k = e - j
+        keep = (r < sizes[atom(0)]) & (s < sizes[atom(j - 1)])
+        if k != 1:
+            keep = keep & (screen[k, atom(j - 1)] == 1)
+        block = jnp.where(keep, go[j], jnp.zeros_like(go[j]))
+        gomat[:, n * width : (n + 1) * width] = mm(order, block).astype(gomat.dtype)
+    for slot in range(2):
+        wait(gvn.at[2 * slot], gv_sems.at[1, slot])
+
+    for e in range(wide):
+        for o in range(band):
+            here = (pl.ds(e * width, width), pl.ds(o * width, width))
+            if not 0 <= e - o < band:
+                gmat[here] = jnp.zeros((width, width), gmat.dtype)
+                continue
+            keep = (r < sizes[atom(e - 2)]) & (s < sizes[atom(o - 1)])
+            if o != 1:
+                keep = keep & (screen[o, atom(0)] == 1)
+            gmat[here] = jnp.where(keep, gvn[o, e - o], jnp.zeros((width, width), gmat.dtype))
+
+    def second_sends(part):
+        for cut in range(2):
+            some = pl.ds(cut * (rows // 4), rows // 4)
+            for dy, dz in PLANE:
+                b = peer(dy, dz)
+                send(
+                    bsend.at[part, b, some], brecv.at[part, blk, some],
+                    b_send_sem, b_recv_sem.at[part], b, ctr,
+                )
+        pltpu.make_async_copy(bsend.at[part, blk], brecv.at[part, blk], b_own_sem.at[part]).start()
+
+    for i in range(2):
+        pgmat[i] = mm(gmat[...], sel[i]).astype(pgmat.dtype)
+
+    def transform(part, carry):
+        slot = lax.rem(part, 2)
+        own_copy(part).wait()
+
+        @pl.when(part + 1 < parts)
+        def _():
+            own_copy(part + 1).start()
+
+        step = 16
+        for j in (1, 0, 2):
+            if j != 1:
+                wait(halo.at[j // 2, part], halo_sems.at[1, j // 2, part])
+
+            def columns(t, carry):
+                at = pl.ds(t * step, step)
+                x = own[slot, at] if j == 1 else halo[j // 2, part, at]
+                for k in range(band):
+                    y = x[:, k].reshape(step * ROWS, width).astype(jnp.float32)
+                    ms[j, k, pl.ds(t * step * ROWS, step * ROWS), :] = y
+                return carry
+
+            lax.fori_loop(0, width // step, columns, 0)
+
+        def green(g, carry):
+            places = [pl.ds(g * AT_ONCE + p, width, stride=ROWS) for p in range(AT_ONCE)]
+            half = []
+            for e in range(wide):
+                js = [n for n, (of, _) in enumerate(terms) if of == e]
+                right = jnp.concatenate(
+                    [
+                        jnp.concatenate(
+                            [
+                                ms[terms[n][1], e - terms[n][1], at, :].astype(jnp.bfloat16)
+                                for at in places
+                            ],
+                            axis=1,
+                        )
+                        for n in js
+                    ],
+                    axis=0,
+                )
+                left = gomat[:, js[0] * width : (js[-1] + 1) * width]
+                half.append(mm(left, right).astype(jnp.bfloat16))
+            both = []
+            for i in range(2):
+                left = jnp.concatenate(
+                    [
+                        jnp.concatenate(
+                            [
+                                h[
+                                    i * half_width : (i + 1) * half_width,
+                                    p * width : (p + 1) * width,
+                                ]
+                                for h in half
+                            ],
+                            axis=1,
+                        )
+                        for p in range(AT_ONCE)
+                    ],
+                    axis=0,
+                )
+                both.append(mm(left, pgmat[i]))
+            for t, v in enumerate(fold(*both)):
+                for p in range(AT_ONCE):
+                    at = pl.ds(g * AT_ONCE + p, half_width, stride=ROWS)
+                    bsc[t, at, :] = v[p * half_width : (p + 1) * half_width]
+            return carry
+
+        lax.fori_loop(0, ROWS // AT_ONCE, green, 0)
+
+        def rounded(i, carry):
+            some = rows // 2
+            for t in range(2 * band - 1):
+                b = bsc[t, pl.ds(i * some * ROWS, some * ROWS), :].astype(jnp.bfloat16)
+                bsend[part, i, :, t] = b.reshape(some, ROWS, width)
+            return carry
+
+        lax.fori_loop(0, nblk, rounded, 0)
+
+        @pl.when(part > 0)
+        def _():
+            second_sends(part - 1)
+
+        return carry
+
+    lax.fori_loop(0, parts, transform, 0)
+
+    wait(mrecv.at[blk], slot_sem)
+    wait(mrecv.at[pl.ds(0, nblk - 1)], m_sems.at[1])
+
+    group = nblk // TILES
+    cols = nblk * ROWS
+    last = parts - 1
+
+    def first(t):
+        return lax.rem(y + t, TILES) * group
+
+    def product(part, sent, got, send_sem):
+        pltpu.make_async_copy(bsend.at[part, blk], brecv.at[part, blk], b_own_sem.at[part]).wait()
+        wait(brecv.at[part, pl.ds(0, nblk - 1)], b_recv_sem.at[part])
+
+        def tile(t, carry):
+            at = pl.ds(first(t), group)
+            here = pl.ds(pl.multiple_of(t * group * 8, group * 8), group * 8)
+            acc = None
+            for m0 in range(0, rows // 2, 2):
+                pairs = [(m, o) for m in (m0, m0 + 1) for o in range(2 * band - 1)]
+                left = jnp.concatenate(
+                    [mrecv[at, m, o].reshape(group * share, width) for m, o in pairs], axis=1
+                )
+                right = jnp.concatenate(
+                    [brecv[part, :, m, o].reshape(cols, width) for m, o in pairs], axis=1
+                )
+                term = mm_nt(left, right)
+                acc = term if acc is None else acc + term
+            acc = acc.reshape(group, nctr, 8, cols)
+            for c in range(nctr):
+                sent[c, here, :] = acc[:, c].reshape(group * 8, cols).astype(sent.dtype)
+            for d in range(1, nctr):
+                c = atom(d)
+                send(
+                    sent.at[c, here, :], got.at[d - 1, here, :],
+                    send_sem, x_recv_sem.at[part, t], blk, c,
+                )
+            return carry
+
+        lax.fori_loop(0, TILES, tile, 0)
+
+    def reduce(part, sent, got):
+        def tile(t, carry):
+            here = pl.ds(pl.multiple_of(t * group * 8, group * 8), group * 8)
+            wait(got.at[:, here, :], x_recv_sem.at[part, t])
+            total = sent[ctr, here, :].astype(jnp.float32)
+            for d in range(nctr - 1):
+                total = total + got[d, here, :].astype(jnp.float32)
+            ysend[part, here, :] = total
+            for i in range(group):
+                b = first(t) + i
+                row = pl.ds(pl.multiple_of((t * group + i) * 8, 8), 8)
+
+                @pl.when(b == blk)
+                def _():
+                    yrecv[part, blk] = ysend[part, row, :]
+
+                @pl.when(b != blk)
+                def _():
+                    send(ysend.at[part, row, :], yrecv.at[part, blk], y_send_sem, y_recv_sem, b, ctr)
+
+            return carry
+
+        lax.fori_loop(0, TILES, tile, 0)
+
+    def middle(part, carry):
+        product(part, xsend.at[part], xrecv.at[part], x_send_sems.at[0])
+
+        @pl.when(part == 1)
+        def _():
+            second_sends(last)
+
+        @pl.when(part > 0)
+        def _():
+            reduce(part - 1, xsend.at[part - 1], xrecv.at[part - 1])
+
+        return carry
+
+    lax.fori_loop(0, last, middle, 0)
+    product(last, xsend_last, xrecv_last, x_send_sems.at[1])
+    reduce(last - 1, xsend.at[last - 1], xrecv.at[last - 1])
+    reduce(last, xsend_last, xrecv_last)
+
+    scale = -2.0 / (width * math.sqrt(nctr * band))
+    wait(yrecv.at[:, pl.ds(0, nblk - 1)], y_recv_sem)
+    lane = lax.broadcasted_iota(jnp.int32, (8, LANES), 1)
+    held = [jnp.zeros((8, LANES), jnp.float32) for _ in range(nblk * share // LANES)]
+    for part in range(parts):
+        total = yrecv[part, 0]
+        for n in range(1, nblk):
+            total = total + yrecv[part, n]
+        total = total * scale
+        for n in range(nblk):
+            at, to = n * ROWS, n * share + part * ROWS
+            piece = total[:, at // LANES * LANES : (at // LANES + 1) * LANES]
+            shift = (to - at) % LANES
+            if shift:
+                piece = pltpu.roll(piece, shift, 1)
+            here = (lane >= to % LANES) & (lane < to % LANES + ROWS)
+            held[to // LANES] = jnp.where(here, piece, held[to // LANES])
+    for n, piece in enumerate(held):
+        out[:, n * LANES : (n + 1) * LANES] = piece
+
+    for slot in range(2):
+        wait(gvn.at[2 * slot], gv_sems.at[0, slot])
+        for part in range(parts):
+            wait(halo.at[slot, part], halo_sems.at[0, slot, part])
+    wait(mrecv.at[pl.ds(0, nblk - 1)], m_sems.at[0])
+    wait(brecv.at[:, pl.ds(0, nblk - 1)], b_send_sem)
+    wait(xrecv, x_send_sems.at[0])
+    wait(xrecv_last, x_send_sems.at[1])
+    wait(yrecv.at[:, pl.ds(0, nblk - 1)], y_send_sem)
+
+
+def run(packed, three_centre, green_occupied, green_virtual, block_sizes, screening):
     _, width, band, share, _ = three_centre.shape
     nblk, nctr = lax.axis_size("blk"), lax.axis_size("ctr")
     parts, rows, cols = share // ROWS, width // nblk, nblk * ROWS
     bf16, f32 = jnp.bfloat16, jnp.float32
     vmem, dma = pltpu.VMEM, pltpu.SemaphoreType.DMA
+    units, tiles = (rows // 2, 2 * band - 1) if packed else (rows, band)
+    one = lambda *a: [vmem(*a)] if packed else []
     return pl.pallas_call(
-        kernel,
+        packed_kernel if packed else kernel,
         out_shape=jax.ShapeDtypeStruct((8, nblk * share), f32),
         in_specs=[
             pl.BlockSpec(memory_space=pl.ANY),
@@ -355,15 +731,18 @@
         scratch_shapes=[
             vmem((2, width, band, ROWS, width), bf16),
             vmem((2, parts, width, band, ROWS, width), bf16),
-            vmem((nblk, rows, band, share, width), bf16),
-            vmem((parts, nblk, rows, band, ROWS, width), bf16),
-            vmem((parts, nblk, rows, band, ROWS, width), bf16),
+            *one((parts, nblk, units, tiles, ROWS, width), bf16),
+            vmem((nblk, units, tiles, share, width), bf16),
+            vmem((parts, nblk, units, tiles, ROWS, width), bf16),
+            vmem((parts, nblk, units, tiles, ROWS, width), bf16),
             vmem((band, width, width), bf16),
             vmem((3, band, width, width), bf16),
             vmem(((2 * band - 1) * width, band * width), bf16),
             vmem((width, band * band * width), bf16),
+            *one((2, band * width, band * width), bf16),
+            *one((2, (2 * band - 1) * width, band * width), bf16),
             vmem((band, band, width * ROWS, width), f32),
-            vmem((band, width * ROWS, width), f32),
+            vmem((tiles, width * ROWS * units // rows, width), f32),
             vmem((parts - 1, nctr, nblk * 8, cols), f32),
             vmem((parts - 1, nctr - 1, nblk * 8, cols), f32),
             vmem((nctr, nblk * 8, cols), bf16),
@@ -385,10 +764,21 @@
             dma,
         ],
         compiler_params=pltpu.CompilerParams(
-            collective_id=0, has_side_effects=True, vmem_limit_bytes=62 << 20
+            collective_id=int(packed), has_side_effects=True, vmem_limit_bytes=62 << 20
         ),
-        name="response",
+        name="response_packed" if packed else "response",
     )(three_centre[0], green_occupied[0], green_virtual[0], block_sizes, screening.T)
+
+
+def per_device(*args):
+    sizes, screen = args[3], args[4]
+    band = screen.shape[1]
+    cols = sum(
+        jnp.where((screen[:, k] == 1) | (k == band // 2), jnp.roll(sizes, band // 2 - k), 0)
+        for k in range(band)
+    )
+    fits = jnp.max(cols) <= (2 * band - 1) * args[0].shape[1] // 2
+    return lax.cond(fits, functools.partial(run, True), functools.partial(run, False), *args)
 
 
 def solution(mesh):

time: 161 us -> 144 us (0.89)
  Pallas kernels: 159 us -> 137 us
  other arithmetic: 0 us -> 2.81 us
    pallas_call x1, Pallas kernels: 159 us -> 137 us  [run(): pl.pallas_call(packed_kernel if packed else kernel, out_shape=jax.ShapeDt...]
    reduce_max x0 -> x1, other arithmetic: none -> 2.81 us  [per_device(): fits = jnp.max(cols) <= (2 * band - 1) * args[0].shape[1] // 2]
    slice x0 -> x2, local copies, waits for them, and re-layouts: none -> 2.11 us  [per_device(): jnp.roll(sizes, band // 2 - k)]
where the time goes in v4:
time: 144 us; the launch traced here: 143 us
  Pallas kernels  137 us (95%)
  other arithmetic  2.81 us (2%)
  local copies, waits for them, and re-layouts  2.73 us (2%)
    pallas_call x1, Pallas kernels, run(): pl.pallas_call(packed_kernel if packed else kernel, out_shape=jax.ShapeDt...  137 us

profile of v4, /device:TPU:1, one launch (start us, length us, event | category | flops | bytes accessed | tf_op | source)
XLA Modules:
  0.0 143.3 jit_solution(9427721983683101493)
XLA Ops:
  0.0 0.8 fusion.4
  0.8 1.3 fusion.3
  2.1 2.8 %fusion.2 = s32[]{:T(128)} fusion(s32[1]{0:T(128)} %get-tuple-element.40, s32[7]{0:T(128)S(1)} %get-tuple-element.42, s32[8,3]{0,1:T(4,128)} %param.11, s32[8]{0:T(128)} %param.10, s32[7]{0:T(128)S(1)} %get-tuple-element.41, s32[1]{0:T(128)} %get-tuple-element.39), kind=kLoop, calls=%fused_computation.4 | loop fusion | flops 71 | bytes 164 | tf_op jit(solution)/shard_map/reduce_max | solution.py:780
  5.6 137.1 %conditional.1 = (f32[8,1024]{1,0:T(8,128)S(1)}) conditional(s32[]{:T(128)} %convert_element_type.3, (bf16[1,128,3,64,128]{4,3,2,1,0:T(8,128)(2,1)}, bf16[1,3,128,128]{3,2,1,0:T(8,128)(2,1)}, bf16[1,3,128,128]{3,2,1,0:T(8,128)(2,1)}, s32[8,3]{0,1:T(4,128)}, s32[8]{0:T(128)}) %tuple.11, (bf16[1,128,3,64,128]{4,3,2,1,0:T(8,128)(2,1)}, ...), branch_computations={%region_1.2_spmd, %region_2.3_spmd} | conditional | bytes 8 | solution.py:781
  5.6 137.1 %response_packed.1 = f32[8,1024]{1,0:T(8,128)S(1)} custom-call(bf16[128,3,64,128]{3,2,1,0:T(8,128)(2,1)} %bitcast.23, bf16[3,128,128]{2,1,0:T(8,128)(2,1)} %bitcast.25, bf16[3,128,128]{2,1,0:T(8,128)(2,1)} %bitcast.27, s32[8]{0:T(128)} %get-tuple-element.36.sizes, s32[3,8]{1,0:T(4,128)} %bitcast.29), custom_call_target="tpu_custom_call" | custom-call | tf_op jit(solution)/shard_map/cond/branch_1_fun/response_packed/pallas_call | solution.py:720
  142.7 0.6 copy.11

commit v5 on v4

--- a/solution.py
+++ b/solution.py
@@ -333,6 +333,17 @@
     wait(xrecv, x_send_sems.at[0])
     wait(xrecv_last, x_send_sems.at[1])
     wait(yrecv.at[:, pl.ds(0, nblk - 1)], y_send_sem)
+
+
+def most_columns(sizes, screen, out):
+    atoms, band = sizes.shape[0], screen.shape[0]
+    most = jnp.int32(0)
+    for a in range(atoms):
+        total = sizes[a]
+        for k in (0, band - 1):
+            total = total + jnp.where(screen[k, a] == 1, sizes[(a + k - 1) % atoms], 0)
+        most = jnp.maximum(most, total)
+    out[0] = most
 
 
 def packed_kernel(
@@ -773,11 +784,14 @@
 def per_device(*args):
     sizes, screen = args[3], args[4]
     band = screen.shape[1]
-    cols = sum(
-        jnp.where((screen[:, k] == 1) | (k == band // 2), jnp.roll(sizes, band // 2 - k), 0)
-        for k in range(band)
-    )
-    fits = jnp.max(cols) <= (2 * band - 1) * args[0].shape[1] // 2
+    cols = pl.pallas_call(
+        most_columns,
+        out_shape=jax.ShapeDtypeStruct((1,), jnp.int32),
+        in_specs=[pl.BlockSpec(memory_space=pltpu.SMEM)] * 2,
+        out_specs=pl.BlockSpec(memory_space=pltpu.SMEM),
+        name="most_columns",
+    )(sizes, screen.T)
+    fits = cols[0] <= (2 * band - 1) * args[0].shape[1] // 2
     return lax.cond(fits, functools.partial(run, True), functools.partial(run, False), *args)
 
 

time: 144 us -> 162 us (1.12)
  Pallas kernels: 137 us -> 160 us
  other arithmetic: 2.81 us -> 0 us
  local copies, waits for them, and re-layouts: 2.73 us -> 0.62 us
    pallas_call x1, Pallas kernels: 137 us -> 159 us  [run(): pl.pallas_call(packed_kernel if packed else kernel, out_shape=jax.ShapeDt...]
    reduce_max x1 -> x0, other arithmetic: 2.81 us -> none  [per_device(): fits = jnp.max(cols) <= (2 * band - 1) * args[0].shape[1] // 2]
    slice x2 -> x0, local copies, waits for them, and re-layouts: 2.11 us -> none  [per_device(): jnp.roll(sizes, band // 2 - k)]
where the time goes in v5:
time: 162 us; the launch traced here: 161 us
  Pallas kernels  160 us (99%)
    pallas_call x1, Pallas kernels, run(): pl.pallas_call(packed_kernel if packed else kernel, out_shape=jax.ShapeDt...  159 us

profile of v5, /device:TPU:1, one launch (start us, length us, event | category | flops | bytes accessed | tf_op | source)
XLA Modules:
  0.0 161.4 jit_solution(7394669620647077682)
XLA Ops:
  0.0 1.2 most_columns.1
  1.9 158.9 %conditional.1 = (f32[8,1024]{1,0:T(8,128)S(1)}) conditional(s32[]{:T(128)} %bitcast.9, (bf16[1,128,3,64,128]{4,3,2,1,0:T(8,128)(2,1)}, bf16[1,3,128,128]{3,2,1,0:T(8,128)(2,1)}, bf16[1,3,128,128]{3,2,1,0:T(8,128)(2,1)}, s32[8,3]{0,1:T(4,128)}, s32[8]{0:T(128)}) %tuple.11, (bf16[1,128,3,64,128]{4,3,2,1,0:T(8,128)(2,1)}, ...), branch_computations={%region_0.0_spmd, %region_1.0_spmd} | conditional | bytes 8 | solution.py:795
  1.9 158.9 %response.1 = f32[8,1024]{1,0:T(8,128)S(1)} custom-call(bf16[128,3,64,128]{3,2,1,0:T(8,128)(2,1)} %bitcast.10, bf16[3,128,128]{2,1,0:T(8,128)(2,1)} %bitcast.12, bf16[3,128,128]{2,1,0:T(8,128)(2,1)} %bitcast.14, s32[8]{0:T(128)} %get-tuple-element.31.sizes, s32[3,8]{1,0:T(4,128)} %bitcast.17), custom_call_target="tpu_custom_call" | custom-call | tf_op jit(solution)/shard_map/cond/branch_0_fun/response/pallas_call | solution.py:731
  160.8 0.6 copy.17

commit v6 on v5

--- a/solution.py
+++ b/solution.py
@@ -13,6 +13,7 @@
 ROWS = 16
 TILES = 4
 LANES = 128
+FOLDS = {2: 5, 4: 11, 1: 3}
 AT_ONCE = 4
 
 PLANE = (
@@ -347,7 +348,7 @@
 
 
 def packed_kernel(
-    tc, go_hbm, gv_hbm, sizes, screen, out,
+    fold_rows, tc, go_hbm, gv_hbm, sizes, screen, out,
     own, halo, msend, mrecv, bsend, brecv, go, gvn, gmat, gomat, sel, pgmat, ms, bsc,
     xsend, xrecv, xsend_last, xrecv_last, ysend, yrecv,
     in_sems, own_sem, slot_sem, gv_sems, halo_sems, m_sems, b_send_sem, b_recv_sem, b_own_sem,
@@ -398,21 +399,33 @@
         pl.semaphore_signal(barrier, inc=1, device_id=(blk, atom(d)), device_id_type=MESH)
 
     at = jnp.int32(0)
-    r = lax.broadcasted_iota(jnp.int32, (width, band * width), 0)
-    s = lax.broadcasted_iota(jnp.int32, (width, band * width), 1)
+    tiles = mrecv.shape[2]
+    units = rows // fold_rows
+    limit = tiles * width // fold_rows
+    spots = [
+        (n * limit // width, n * limit % width, -(-(n * limit % width + limit) // width))
+        for n in range(fold_rows)
+    ]
+    r = lax.broadcasted_iota(jnp.int32, (width, sel.shape[2]), 0)
+    s = lax.broadcasted_iota(jnp.int32, (width, sel.shape[2]), 1)
     for o in range(band):
         length = sizes[atom(o - 1)]
         if o != 1:
             length = jnp.where(screen[o, atom(0)] == 1, length, 0)
-        for i in range(2):
-            here = (s - r == at + i * (width // 2)) & (r < length)
-            sel[i, o * width : (o + 1) * width, :] = jnp.where(here, 1.0, 0.0).astype(sel.dtype)
+        for i, (_, lane, span) in enumerate(spots):
+            sel[i, o * width : (o + 1) * width, : span * width] = jnp.where(
+                (s - r == at + lane) & (r < length), 1.0, 0.0
+            ).astype(sel.dtype)[:, : span * width]
         at = at + length
 
-    def fold(even, odd):
-        cut = lambda v: [v[:, n * width : (n + 1) * width] for n in range(band)]
-        even, odd = cut(even), cut(odd)
-        return [*even[:-1], even[-1] + odd[0], *odd[1:]]
+    def fold(values):
+        folded = [None] * tiles
+        for (start, _, span), v in zip(spots, values):
+            for n in range(span):
+                piece = v[:, n * width : (n + 1) * width]
+                before = folded[start + n]
+                folded[start + n] = piece if before is None else before + piece
+        return folded
 
     def pack(part):
         slot = lax.rem(part, 2)
@@ -424,16 +437,19 @@
 
         def some(g, carry):
             x = own[slot, pl.ds(g * 4 * rows, 4 * rows)]
-            x = x.reshape(2 * rows, 2, band, ROWS, width)
-            even, odd = (
-                jnp.concatenate(
-                    [x[:, i, n].reshape(2 * rows * ROWS, width) for n in range(band)], axis=1
-                )
-                for i in range(2)
-            )
-            for t, v in enumerate(fold(mm(even, sel[0]), mm(odd, sel[1]))):
+            x = x.reshape(4 * units, fold_rows, band, ROWS, width)
+            values = [
+                mm(
+                    jnp.concatenate(
+                        [x[:, i, n].reshape(4 * units * ROWS, width) for n in range(band)], axis=1
+                    ),
+                    sel[i, :, : spots[i][2] * width],
+                )
+                for i in range(fold_rows)
+            ]
+            for t, v in enumerate(fold(values)):
                 msend[part, pl.ds(g * 4, 4), :, t] = v.astype(jnp.bfloat16).reshape(
-                    4, rows // 2, ROWS, width
+                    4, units, ROWS, width
                 )
             return carry
 
@@ -460,7 +476,7 @@
             pack(part)
 
         for cut in range(2):
-            some = pl.ds(cut * (rows // 4), rows // 4)
+            some = pl.ds(cut * (units // 2), units // 2)
             for dy, dz in PLANE:
                 b = peer(dy, dz)
                 send(
@@ -481,8 +497,10 @@
     s = lax.broadcasted_iota(jnp.int32, (width, width), 1)
     for copy in inputs:
         copy.wait()
-    half_width = width // 2
-    place = jnp.where(r < half_width, 2 * r, 2 * (r - half_width) + 1)
+    height = width // fold_rows
+    place = fold_rows * r
+    for n in range(1, fold_rows):
+        place = place - jnp.where(r >= n * height, width - 1, 0)
     order = jnp.where(s == place, 1.0, 0.0).astype(jnp.bfloat16)
     for n, (e, j) in enumerate(terms):
         k = e - j
@@ -507,7 +525,7 @@
 
     def second_sends(part):
         for cut in range(2):
-            some = pl.ds(cut * (rows // 4), rows // 4)
+            some = pl.ds(cut * (units // 2), units // 2)
             for dy, dz in PLANE:
                 b = peer(dy, dz)
                 send(
@@ -516,8 +534,8 @@
                 )
         pltpu.make_async_copy(bsend.at[part, blk], brecv.at[part, blk], b_own_sem.at[part]).start()
 
-    for i in range(2):
-        pgmat[i] = mm(gmat[...], sel[i]).astype(pgmat.dtype)
+    for i, (_, _, span) in enumerate(spots):
+        pgmat[i, :, : span * width] = mm(gmat[...], sel[i, :, : span * width]).astype(pgmat.dtype)
 
     def transform(part, carry):
         slot = lax.rem(part, 2)
@@ -563,13 +581,13 @@
                 left = gomat[:, js[0] * width : (js[-1] + 1) * width]
                 half.append(mm(left, right).astype(jnp.bfloat16))
             both = []
-            for i in range(2):
+            for i in range(fold_rows):
                 left = jnp.concatenate(
                     [
                         jnp.concatenate(
                             [
                                 h[
-                                    i * half_width : (i + 1) * half_width,
+                                    i * height : (i + 1) * height,
                                     p * width : (p + 1) * width,
                                 ]
                                 for h in half
@@ -580,20 +598,19 @@
                     ],
                     axis=0,
                 )
-                both.append(mm(left, pgmat[i]))
-            for t, v in enumerate(fold(*both)):
+                both.append(mm(left, pgmat[i, :, : spots[i][2] * width]))
+            for t, v in enumerate(fold(both)):
                 for p in range(AT_ONCE):
-                    at = pl.ds(g * AT_ONCE + p, half_width, stride=ROWS)
-                    bsc[t, at, :] = v[p * half_width : (p + 1) * half_width]
+                    at = pl.ds(g * AT_ONCE + p, height, stride=ROWS)
+                    bsc[t, at, :] = v[p * height : (p + 1) * height]
             return carry
 
         lax.fori_loop(0, ROWS // AT_ONCE, green, 0)
 
         def rounded(i, carry):
-            some = rows // 2
-            for t in range(2 * band - 1):
-                b = bsc[t, pl.ds(i * some * ROWS, some * ROWS), :].astype(jnp.bfloat16)
-                bsend[part, i, :, t] = b.reshape(some, ROWS, width)
+            for t in range(tiles):
+                b = bsc[t, pl.ds(i * units * ROWS, units * ROWS), :].astype(jnp.bfloat16)
+                bsend[part, i, :, t] = b.reshape(units, ROWS, width)
             return carry
 
         lax.fori_loop(0, nblk, rounded, 0)
@@ -624,8 +641,9 @@
             at = pl.ds(first(t), group)
             here = pl.ds(pl.multiple_of(t * group * 8, group * 8), group * 8)
             acc = None
-            for m0 in range(0, rows // 2, 2):
-                pairs = [(m, o) for m in (m0, m0 + 1) for o in range(2 * band - 1)]
+            step = 4 // fold_rows
+            for m0 in range(0, units, step):
+                pairs = [(m, o) for m in range(m0, m0 + step) for o in range(tiles)]
                 left = jnp.concatenate(
                     [mrecv[at, m, o].reshape(group * share, width) for m, o in pairs], axis=1
                 )
@@ -720,16 +738,19 @@
     wait(yrecv.at[:, pl.ds(0, nblk - 1)], y_send_sem)
 
 
-def run(packed, three_centre, green_occupied, green_virtual, block_sizes, screening):
+def run(fold_rows, three_centre, green_occupied, green_virtual, block_sizes, screening):
     _, width, band, share, _ = three_centre.shape
     nblk, nctr = lax.axis_size("blk"), lax.axis_size("ctr")
     parts, rows, cols = share // ROWS, width // nblk, nblk * ROWS
     bf16, f32 = jnp.bfloat16, jnp.float32
     vmem, dma = pltpu.VMEM, pltpu.SemaphoreType.DMA
-    units, tiles = (rows // 2, 2 * band - 1) if packed else (rows, band)
+    packed = fold_rows > 1
+    units, tiles = rows // fold_rows, FOLDS[fold_rows]
+    early = bf16 if fold_rows > 2 else f32
+    reach = (fold_rows // 2 + 2) * width
     one = lambda *a: [vmem(*a)] if packed else []
     return pl.pallas_call(
-        packed_kernel if packed else kernel,
+        functools.partial(packed_kernel, fold_rows) if packed else kernel,
         out_shape=jax.ShapeDtypeStruct((8, nblk * share), f32),
         in_specs=[
             pl.BlockSpec(memory_space=pl.ANY),
@@ -750,12 +771,12 @@
             vmem((3, band, width, width), bf16),
             vmem(((2 * band - 1) * width, band * width), bf16),
             vmem((width, band * band * width), bf16),
-            *one((2, band * width, band * width), bf16),
-            *one((2, (2 * band - 1) * width, band * width), bf16),
+            *one((fold_rows, band * width, reach), bf16),
+            *one((fold_rows, (2 * band - 1) * width, reach), bf16),
             vmem((band, band, width * ROWS, width), f32),
             vmem((tiles, width * ROWS * units // rows, width), f32),
-            vmem((parts - 1, nctr, nblk * 8, cols), f32),
-            vmem((parts - 1, nctr - 1, nblk * 8, cols), f32),
+            vmem((parts - 1, nctr, nblk * 8, cols), early),
+            vmem((parts - 1, nctr - 1, nblk * 8, cols), early),
             vmem((nctr, nblk * 8, cols), bf16),
             vmem((nctr - 1, nblk * 8, cols), bf16),
             vmem((parts, nblk * 8, cols), f32),
@@ -775,9 +796,9 @@
             dma,
         ],
         compiler_params=pltpu.CompilerParams(
-            collective_id=int(packed), has_side_effects=True, vmem_limit_bytes=62 << 20
+            collective_id=list(FOLDS).index(fold_rows), has_side_effects=True, vmem_limit_bytes=62 << 20
         ),
-        name="response_packed" if packed else "response",
+        name="response_%d" % fold_rows,
     )(three_centre[0], green_occupied[0], green_virtual[0], block_sizes, screening.T)
 
 
@@ -791,8 +812,10 @@
         out_specs=pl.BlockSpec(memory_space=pltpu.SMEM),
         name="most_columns",
     )(sizes, screen.T)
-    fits = cols[0] <= (2 * band - 1) * args[0].shape[1] // 2
-    return lax.cond(fits, functools.partial(run, True), functools.partial(run, False), *args)
+    width = args[0].shape[1]
+    limits = {f: t * width // f for f, t in FOLDS.items() if f > 1}
+    branch = sum((cols[0] > limit).astype(jnp.int32) for limit in limits.values())
+    return lax.switch(branch, [functools.partial(run, f) for f in (*limits, 1)], *args)
 
 
 def solution(mesh):

time: 162 us -> 141 us (0.87)
  Pallas kernels: 160 us -> 138 us
    pallas_call x1, Pallas kernels: 159 us -> 137 us  [run(): pl.pallas_call(functools.partial(packed_kernel, fold_rows) if packed else...]
where the time goes in v6:
time: 141 us; the launch traced here: 140 us
  Pallas kernels  138 us (98%)
    pallas_call x1, Pallas kernels, run(): pl.pallas_call(functools.partial(packed_kernel, fold_rows) if packed else...  137 us

profile of v6, /device:TPU:1, one launch (start us, length us, event | category | flops | bytes accessed | tf_op | source)
XLA Modules:
  0.0 140.5 jit_solution(7490716881507501250)
XLA Ops:
  0.0 1.2 most_columns.1
  2.5 137.3 %conditional.1 = (f32[8,1024]{1,0:T(8,128)S(1)}) conditional(s32[]{:T(128)} %bitcast.13, (bf16[1,128,3,64,128]{4,3,2,1,0:T(8,128)(2,1)}, bf16[1,3,128,128]{3,2,1,0:T(8,128)(2,1)}, bf16[1,3,128,128]{3,2,1,0:T(8,128)(2,1)}, s32[8,3]{0,1:T(4,128)}, s32[8]{0:T(128)}) %tuple.14, (bf16[1,128,3,64,128]{4,3,2,1,0:T(8,128)(2,1)}, ...), branch_computations={%region_0.0_spmd, %region_1.0_spmd, %region_2.0_spmd} | conditional | bytes 8 | solution.py:818
  2.6 137.1 %response_2.1 = f32[8,1024]{1,0:T(8,128)S(1)} custom-call(bf16[128,3,64,128]{3,2,1,0:T(8,128)(2,1)} %bitcast.14, bf16[3,128,128]{2,1,0:T(8,128)(2,1)} %bitcast.17, bf16[3,128,128]{2,1,0:T(8,128)(2,1)} %bitcast.20, s32[8]{0:T(128)} %get-tuple-element.42.sizes, s32[3,8]{1,0:T(4,128)} %bitcast.24), custom_call_target="tpu_custom_call" | custom-call | tf_op jit(solution)/shard_map/cond/branch_0_fun/response_2/pallas_call | solution.py:752
  139.9 0.6 copy.22

commit v7 on v6

--- a/solution.py
+++ b/solution.py
@@ -746,7 +746,7 @@
     vmem, dma = pltpu.VMEM, pltpu.SemaphoreType.DMA
     packed = fold_rows > 1
     units, tiles = rows // fold_rows, FOLDS[fold_rows]
-    early = bf16 if fold_rows > 2 else f32
+    early = bf16
     reach = (fold_rows // 2 + 2) * width
     one = lambda *a: [vmem(*a)] if packed else []
     return pl.pallas_call(

time: 141 us -> 141 us (level)
  no operation moved by 1% of the time
where the time goes in v7:
time: 141 us; the launch traced here: 140 us
  Pallas kernels  138 us (98%)
    pallas_call x1, Pallas kernels, run(): pl.pallas_call(functools.partial(packed_kernel, fold_rows) if packed else...  137 us

profile of v7, /device:TPU:1, one launch (start us, length us, event | category | flops | bytes accessed | tf_op | source)
XLA Modules:
  0.0 140.5 jit_solution(5318287444524418116)
XLA Ops:
  0.0 1.2 most_columns.1
  2.5 137.3 %conditional.1 = (f32[8,1024]{1,0:T(8,128)S(1)}) conditional(s32[]{:T(128)} %bitcast.13, (bf16[1,128,3,64,128]{4,3,2,1,0:T(8,128)(2,1)}, bf16[1,3,128,128]{3,2,1,0:T(8,128)(2,1)}, bf16[1,3,128,128]{3,2,1,0:T(8,128)(2,1)}, s32[8,3]{0,1:T(4,128)}, s32[8]{0:T(128)}) %tuple.14, (bf16[1,128,3,64,128]{4,3,2,1,0:T(8,128)(2,1)}, ...), branch_computations={%region_0.0_spmd, %region_1.0_spmd, %region_2.0_spmd} | conditional | bytes 8 | solution.py:818
  2.6 137.1 %response_2.1 = f32[8,1024]{1,0:T(8,128)S(1)} custom-call(bf16[128,3,64,128]{3,2,1,0:T(8,128)(2,1)} %bitcast.14, bf16[3,128,128]{2,1,0:T(8,128)(2,1)} %bitcast.17, bf16[3,128,128]{2,1,0:T(8,128)(2,1)} %bitcast.20, s32[8]{0:T(128)} %get-tuple-element.42.sizes, s32[3,8]{1,0:T(4,128)} %bitcast.24), custom_call_target="tpu_custom_call" | custom-call | tf_op jit(solution)/shard_map/cond/branch_0_fun/response_2/pallas_call | solution.py:752
  139.9 0.6 copy.22
